TPU v7x, 32 devices: a whole 2x2x4 slice. The times are simulated.
32 devices in a mesh: row: 4 (over z), col: 8 (over y, x, core).
Axes of the slice: x: 2, y: 2, z: 4, core: 2. Of those that a mesh axis runs over, the one named last changes fastest.
Arguments:
- snapshots: float32 [128, 49152], P(('row', 'col')), may hold values from -6 to 6
- panels: float32 [8, 6, 8192, 256], P(None, None, ('row', 'col')), may hold values from -0.1875 to 0.1875
- diag_inverse: float32 [8, 256, 256], replicated, may hold values from -0.6 to 1.5, as said below
Outputs:
- whitened: float32 [6, 8192, 128], P(None, ('row', 'col'))
Inputs may be any that keep to these rules, and one draw needn't show every extreme that they name: Each block of diag_inverse is lower triangular with a diagonal of 0.5 to 1.5.
All inputs are finite; a program needn't handle non-finite values.
Results may differ from a plain program's by a relative error of at most 0.0001.
Values sent between devices are 32-bit elements; how exact they have to be, the bound alone decides.
A program may use at most 128 MiB of HBM per device.

v0:
```python
import jax
import jax.numpy as jnp
from jax import lax
from jax.sharding import PartitionSpec as P


def spread(block, axis, owner):
    block = jnp.where(lax.axis_index(axis) == owner, block, jnp.zeros_like(block))
    return lax.psum(block, axis)


def per_device(snapshots, panels, diag_inverse):
    local_count, order_size = snapshots.shape
    sections, blocks, width_block, _ = panels.shape
    devices = lax.axis_size(("row", "col"))
    pieces = snapshots.reshape(local_count, blocks, devices, width_block)
    arrived = lax.all_to_all(pieces, ("row", "col"), split_axis=2, concat_axis=0, tiled=True)
    remaining = jnp.transpose(
        arrived.reshape(devices * local_count, blocks, width_block), (1, 2, 0)
    )
    device = lax.axis_index(("row", "col"))
    block_owner = lax.broadcasted_iota(jnp.int32, (blocks, 1, 1), 0) * devices + device
    for section in range(sections):
        solved = jnp.dot(
            diag_inverse[section],
            remaining[0],
            precision=lax.Precision.HIGHEST,
            preferred_element_type=jnp.float32,
        )
        solved = spread(solved, ("row", "col"), section)
        product = jnp.einsum(
            "jrc,cs->jrs",
            panels[section],
            solved,
            precision=lax.Precision.HIGHEST,
            preferred_element_type=jnp.float32,
        )
        remaining = jnp.where(
            block_owner > section,
            remaining - product,
            jnp.where(block_owner == section, solved[None], remaining),
        )
    return remaining


def solution(mesh):
    in_specs = (P(("row", "col"), None), P(None, None, ("row", "col"), None), P())
    out_specs = P(None, ("row", "col"), None)
    return jax.shard_map(
        per_device, mesh=mesh, in_specs=in_specs, out_specs=out_specs, check_vma=False
    )
```

profile of v0, /device:TPU:25, one launch (start us, length us, event | category | flops | bytes accessed | tf_op | source)
XLA Modules:
  0.0 1057.6 jit_solution(2101254170668094777)
XLA Ops:
  9.2 6.2 all-to-all-start
  15.5 18.0 %all-to-all-done = f32[4,6,32,256]{3,0,1,2:T(4,128)S(1)} async-done(((f32[4,6,32,256]{3,0,1,2:T(4,128)}), f32[4,6,32,256]{3,0,1,2:T(4,128)S(1)}, u32[]{:S(2)}, u32[]{:S(2)}) %all-to-all-start) | async-done | bytes 786464 | tf_op jit(solution)/shard_map/all_to_all | solution.py:17
  36.0 120.9 %all-reduce.9.cloned.1.call-done = f32[256,128]{1,0:T(8,128)} async-done(((f32[256,128]{1,0:T(8,128)}), f32[256,128]{1,0:T(8,128)}) %all-reduce.9.cloned.1.call-update) | async-done | bytes 131088 | tf_op jit(solution)/shard_map/psum | solution.py:9
  157.9 3.0 fusion.93
  162.9 121.6 %all-reduce.11.cloned.1.call-done = f32[256,128]{0,1:T(8,128)} async-done(((f32[256,128]{0,1:T(8,128)}), f32[256,128]{0,1:T(8,128)}) %all-reduce.11.cloned.1.call-update) | async-done | bytes 131088 | tf_op jit(solution)/shard_map/psum | solution.py:9
  284.5 3.1 fusion.87
  287.7 2.0 fusion.101
  289.8 121.8 %all-reduce.13.cloned.1.call-done = f32[256,128]{0,1:T(8,128)} async-done(((f32[256,128]{0,1:T(8,128)}), f32[256,128]{0,1:T(8,128)}) %all-reduce.13.cloned.1.call-update) | async-done | bytes 131088 | tf_op jit(solution)/shard_map/psum | solution.py:9
  411.6 3.1 fusion.81
  414.7 2.0 fusion.100
  416.8 121.7 %all-reduce.15.cloned.1.call-done = f32[256,128]{0,1:T(8,128)} async-done(((f32[256,128]{0,1:T(8,128)}), f32[256,128]{0,1:T(8,128)}) %all-reduce.15.cloned.1.call-update) | async-done | bytes 131088 | tf_op jit(solution)/shard_map/psum | solution.py:9
  538.5 3.1 fusion.75
  541.6 2.0 fusion.99
  543.7 121.7 %all-reduce.17.cloned.1.call-done = f32[256,128]{0,1:T(8,128)} async-done(((f32[256,128]{0,1:T(8,128)}), f32[256,128]{0,1:T(8,128)}) %all-reduce.17.cloned.1.call-update) | async-done | bytes 131088 | tf_op jit(solution)/shard_map/psum | solution.py:9
  665.4 3.1 fusion.69
  668.6 2.0 fusion.98
  670.8 121.5 %all-reduce.19.cloned.1.call-done = f32[256,128]{0,1:T(8,128)} async-done(((f32[256,128]{0,1:T(8,128)}), f32[256,128]{0,1:T(8,128)}) %all-reduce.19.cloned.1.call-update) | async-done | bytes 131088 | tf_op jit(solution)/shard_map/psum | solution.py:9
  792.3 3.1 fusion.63
  795.5 2.0 fusion.97
  797.6 121.8 %all-reduce.21.cloned.1.call-done = f32[256,128]{0,1:T(8,128)} async-done(((f32[256,128]{0,1:T(8,128)}), f32[256,128]{0,1:T(8,128)}) %all-reduce.21.cloned.1.call-update) | async-done | bytes 131088 | tf_op jit(solution)/shard_map/psum | solution.py:9
  919.4 3.1 fusion.57
  922.5 2.0 fusion.96
  924.6 121.9 %all-reduce.23.cloned.1.call-done = f32[256,128]{0,1:T(8,128)} async-done(((f32[256,128]{0,1:T(8,128)}), f32[256,128]{0,1:T(8,128)}) %all-reduce.23.cloned.1.call-update) | async-done | bytes 131088 | tf_op jit(solution)/shard_map/psum | solution.py:9
  1046.5 3.1 fusion.51
  (32 shorter events, 9.9 us)
Async XLA Ops:
  9.2 24.2 %all-to-all-start = ((f32[4,6,32,256]{3,0,1,2:T(4,128)}), f32[4,6,32,256]{3,0,1,2:T(4,128)S(1)}, u32[]{:S(2)}, u32[]{:S(2)}) async-start(f32[4,6,32,256]{3,0,1,2:T(4,128)} %copy.12), calls=%async_computation | async-start | bytes 1572864 | tf_op jit(solution)/shard_map/all_to_all | solution.py:17
  15.4 141.4 %all-reduce.9.cloned.1.call-start = ((), (), s32[]{:S(2)}) async-start(), calls=%async_computation.1 | async-start | bytes 262144 | tf_op jit(solution)/shard_map/psum | solution.py:9
  35.9 248.6 %all-reduce.11.cloned.1.call-start = ((), (), s32[]{:S(2)}) async-start(), calls=%async_computation.2 | async-start | bytes 262144 | tf_op jit(solution)/shard_map/psum | solution.py:9
  162.9 248.7 %all-reduce.13.cloned.1.call-start = ((), (), s32[]{:S(2)}) async-start(), calls=%async_computation.3 | async-start | bytes 262144 | tf_op jit(solution)/shard_map/psum | solution.py:9
  289.7 248.8 %all-reduce.15.cloned.1.call-start = ((), (), s32[]{:S(2)}) async-start(), calls=%async_computation.4 | async-start | bytes 262144 | tf_op jit(solution)/shard_map/psum | solution.py:9
  416.8 248.7 %all-reduce.17.cloned.1.call-start = ((), (), s32[]{:S(2)}) async-start(), calls=%async_computation.5 | async-start | bytes 262144 | tf_op jit(solution)/shard_map/psum | solution.py:9
  543.7 248.6 %all-reduce.19.cloned.1.call-start = ((), (), s32[]{:S(2)}) async-start(), calls=%async_computation.6 | async-start | bytes 262144 | tf_op jit(solution)/shard_map/psum | solution.py:9
  670.6 248.8 %all-reduce.21.cloned.1.call-start = ((), (), s32[]{:S(2)}) async-start(), calls=%async_computation.7 | async-start | bytes 262144 | tf_op jit(solution)/shard_map/psum | solution.py:9
  797.5 248.9 %all-reduce.23.cloned.1.call-start = ((), (), s32[]{:S(2)}) async-start(), calls=%async_computation.8 | async-start | bytes 262144 | tf_op jit(solution)/shard_map/psum | solution.py:9
Sparse Core Ops, SparseCore 0:
  36.0 120.7 all-reduce.8
  163.0 121.4 all-reduce.10
  290.1 121.4 all-reduce.12
  417.0 121.4 all-reduce.14
  543.9 121.4 all-reduce.16
  670.8 121.4 all-reduce.18
  797.9 121.4 all-reduce.20
  924.9 121.4 all-reduce.22
where the time goes:
time: 1060 us
  waiting for transfers between devices  991 us (93%)
  matrix products  41 us (4%)
  between operations  13.7 us (1%)
    psum x8, waiting for transfers between devices, spread(): return lax.psum(block, axis)  973 us
    dot_general x8, matrix products, per_device(): jnp.einsum('jrc,cs->jrs', panels[section], solved, precision=lax.Precisio...  25 us
  transfers between devices with their start and end apart: 9, of which 9 were waited for; matrix products, arithmetic and copies ran while one was open for 0% of the time, Pallas kernels for 0%

commit v1 on v0

v1 whole, which is shorter than its diff:
```python
import functools

import jax
import jax.numpy as jnp
from jax import lax
from jax.experimental import pallas as pl
from jax.experimental.pallas import tpu as pltpu
from jax.sharding import PartitionSpec as P

MESH = pl.DeviceIdType.MESH
NT = (((1,), (1,)), ((), ()))
NN = (((1,), (0,)), ((), ()))


def halves(value):
    high = value.astype(jnp.bfloat16)
    low = (value - high.astype(jnp.float32)).astype(jnp.bfloat16)
    return high, low


def mul(a, b, dims):
    return lax.dot_general(a, b, dims, preferred_element_type=jnp.float32)


def product(a, b_high, b_low, dims):
    rows = a.shape[0]
    a_high, a_low = halves(a)
    both = mul(jnp.concatenate([a_high, a_low], axis=0), b_high, dims)
    return both[:rows] + (both[rows:] + mul(a_high, b_low, dims))


def kernel(
    rows, cols, snap, panels, diag, out,
    recv, first, solved, strip, strip_high, strip_low, inverse_high, inverse_low,
    diagonal, lead, staged, high, low, both, total, piled,
    a2a_send, a2a_recv, first_send, first_recv, strip_send, strip_recv, strip_own, diag_sem,
    staged_sem, half_send, half_recv, partner_send, up_send, piece_recv, plane_send,
):
    devices = rows * cols
    groups = cols // 2
    steps, blocks, width, _ = panels.shape
    stages = steps // 2
    count = out.shape[2]
    half_count = count // 2
    local = snap.shape[3]
    half_devices = devices // 2

    row = lax.axis_index("row")
    col = lax.axis_index("col")
    me = row * cols + col
    group = col // 2
    side = col % 2
    in_chain = me < steps

    def device(index):
        return (index // cols, index % cols)

    def remote(src, dst, send, recv_sem, target):
        return pltpu.make_async_remote_copy(
            src_ref=src, dst_ref=dst, send_sem=send, recv_sem=recv_sem,
            device_id=target, device_id_type=MESH,
        )

    def arrived(ref, sem):
        pltpu.make_async_copy(ref, ref, sem).wait()

    def strip_local(k):
        return pltpu.make_async_copy(panels.at[k, 0], strip.at[side, k], strip_own.at[k])

    def diag_copy():
        return pltpu.make_async_copy(diag.at[pl.ds(2 * group, 2)], diagonal, diag_sem)

    def staged_copy(k):
        return pltpu.make_async_copy(panels.at[k], staged.at[k], staged_sem.at[k])

    @pl.when(in_chain)
    def _():
        diag_copy().start()
        for k in range(steps - 1):
            @pl.when(k < me)
            def _():
                strip_local(k).start()

    for k in range(steps):
        staged_copy(k).start()

    barrier = pltpu.get_barrier_semaphore()

    def greet(i, carry):
        pl.semaphore_signal(
            barrier, inc=1, device_id=device((me + i) % devices), device_id_type=MESH
        )
        return carry

    lax.fori_loop(1, devices, greet, 0)
    pl.semaphore_wait(barrier, devices - 1)

    my_half = me // half_devices
    place = me % half_devices

    def first_remote(c):
        return remote(
            snap.at[0, pl.ds(2 * c, 2)], first.at[place], first_send.at[c],
            first_recv.at[place], device(2 * c + my_half),
        )

    def first_local(c):
        return pltpu.make_async_copy(
            snap.at[0, pl.ds(2 * c, 2)], first.at[place], first_recv.at[place]
        )

    for c in range(stages):
        @pl.when(2 * c + my_half != me)
        def _():
            first_remote(c).start()

        @pl.when(2 * c + my_half == me)
        def _():
            first_local(c).start()

    partner = (row, 2 * group + 1 - side)

    def strip_remote(k):
        return remote(
            panels.at[k, 0], strip.at[side, k], strip_send.at[k], strip_recv.at[k], partner
        )

    @pl.when(in_chain)
    def _():
        for k in reversed(range(steps - 1)):
            @pl.when(k < me)
            def _():
                strip_remote(k).start()

    def a2a_lead(target):
        return remote(
            snap.at[pl.ds(1, blocks - 1), target], recv.at[me, pl.ds(1, blocks - 1)],
            a2a_send.at[target], a2a_recv.at[me], device(target),
        )

    def a2a_rest(target):
        return remote(
            snap.at[:, target], recv.at[me], a2a_send.at[target], a2a_recv.at[me], device(target)
        )

    def a2a_start(i, carry):
        target = (me + i) % devices

        @pl.when(target < steps)
        def _():
            a2a_lead(target).start()

        @pl.when(target >= steps)
        def _():
            a2a_rest(target).start()

        return carry

    lax.fori_loop(1, devices, a2a_start, 0)
    own_copy = pltpu.make_async_copy(snap.at[:, me], recv.at[me], a2a_recv.at[me])
    own_copy.start()

    def split_all():
        for k in range(steps):
            staged_copy(k).wait()

        def one(i, carry):
            s, j = i // blocks, i % blocks
            for t in range(2):
                h, l = halves(staged[2 * s + t, j])
                high[s, j, :, t * width:(t + 1) * width] = h
                low[s, j, :, t * width:(t + 1) * width] = l
            return carry

        lax.fori_loop(0, stages * blocks, one, 0)

    early = jnp.logical_or(me >= steps, me >= steps // 2)

    def half_ref(s, which):
        return solved.at[s, pl.ds(which * groups, groups)]

    mine = side * groups + group

    def to_partner(s):
        return remote(
            half_ref(s, side), half_ref(s, side), partner_send.at[s],
            half_recv.at[s, side], partner,
        )

    def upward(s, r):
        return remote(
            solved.at[s, mine], solved.at[s, mine], up_send.at[s, r - 1],
            piece_recv.at[s, mine], (r, col),
        )

    def forward(s):
        for r in range(1, rows):
            upward(s, r).start()
        to_partner(s).start()

    def across(s, g):
        return remote(
            half_ref(s, side), half_ref(s, side), half_send.at[g],
            half_recv.at[s, side], (row, 2 * g + side),
        )

    def in_plane(s, i):
        target = (col + i) % cols
        return remote(
            solved.at[s, mine], solved.at[s, mine], plane_send.at[s, i - 1],
            piece_recv.at[s, mine], (row, target),
        )

    @pl.when(early)
    def _():
        split_all()

    @pl.when(in_chain)
    def _():
        diag_copy().wait()
        for k in range(steps - 1):
            @pl.when(k < me)
            def _():
                strip_local(k).wait()

            @pl.when(k < 2 * group + 1 - side)
            def _():
                arrived(strip.at[1 - side, k], strip_recv.at[k])

        d0, d1 = diagonal[0], diagonal[1]
        d0_high, d0_low = halves(d0)
        below = strip[1, 2 * group]
        inner = product(below, d0_high, d0_low, NN)
        inner_high, inner_low = halves(inner)
        corner = -product(d1, inner_high, inner_low, NN)
        for r0, c0, value in (
            (0, 0, d0), (0, width, jnp.zeros_like(d0)), (width, 0, corner), (width, width, d1)
        ):
            h, l = halves(value)
            inverse_high[r0:r0 + width, c0:c0 + width] = h
            inverse_low[r0:r0 + width, c0:c0 + width] = l
        for s in range(stages - 1):
            @pl.when(s < group)
            def _():
                for b in range(2):
                    for t in range(2):
                        h, l = halves(strip[b, 2 * s + t])
                        place_ = (s, slice(b * width, (b + 1) * width), slice(t * width, (t + 1) * width))
                        strip_high[place_] = h
                        strip_low[place_] = l

        def first_wait(i, carry):
            arrived(first.at[i], first_recv.at[i])
            return carry

        lax.fori_loop(0, half_devices, first_wait, 0)

        def pile(i, carry):
            at = pl.ds(pl.multiple_of(i * 2 * local, 2 * local), 2 * local)
            for b in range(2):
                for t in range(width // 128):
                    lanes = slice(b * width + t * 128, b * width + (t + 1) * 128)
                    lead[at, lanes] = jnp.concatenate(
                        [first[2 * i, b, t], first[2 * i + 1, b, t]], axis=0
                    )
            return carry

        lax.fori_loop(0, half_devices // 2, pile, 0)

        for s in range(stages):
            @pl.when(s < group)
            def _():
                arrived(half_ref(s, side), half_recv.at[s, side])
                forward(s)
                x = half_ref(s, side)[...].reshape(half_count, 2 * width)
                lead[...] -= product(x, strip_high[min(s, stages - 2)], strip_low[min(s, stages - 2)], NT)

            @pl.when(s == group)
            def _():
                x = product(lead[...], inverse_high[...], inverse_low[...], NT)
                half_ref(s, side)[...] = x.reshape(groups, half_count // groups, 2 * width)
                for i in range(1, groups):
                    across(s, (s + i) % groups).start()
                forward(s)

    @pl.when(jnp.logical_not(early))
    def _():
        split_all()

    for s in range(stages):
        @pl.when(row == 0)
        def _():
            @pl.when(jnp.logical_or(jnp.logical_not(in_chain), s > group))
            def _():
                arrived(half_ref(s, side), half_recv.at[s, side])
                forward(s)

            arrived(half_ref(s, 1 - side), half_recv.at[s, 1 - side])

        @pl.when(row > 0)
        def _():
            arrived(solved.at[s, mine], piece_recv.at[s, mine])
            for i in range(1, cols):
                in_plane(s, i).start()
            for i in range(1, cols):
                other = (col + i) % cols
                piece = (other % 2) * groups + other // 2
                arrived(solved.at[s, piece], piece_recv.at[s, piece])

        x_high, x_low = halves(solved[s].reshape(count, 2 * width))
        both[:count] = x_high
        both[count:] = x_low

        def update(j, carry):
            a = mul(high[s, j], both[...], NT)
            b = mul(low[s, j], both[:count], NT)
            term = a[:, :count] + (a[:, count:] + b)
            if s == 0:
                total[j] = term
            else:
                total[j] += term
            return carry

        lax.fori_loop(0, blocks, update, 0)

    own_copy.wait()

    def a2a_wait(i, carry):
        source = (me + i) % devices

        @pl.when(in_chain)
        def _():
            arrived(recv.at[source, pl.ds(1, blocks - 1)], a2a_recv.at[source])

        @pl.when(jnp.logical_not(in_chain))
        def _():
            arrived(recv.at[source], a2a_recv.at[source])

        return carry

    lax.fori_loop(1, devices, a2a_wait, 0)

    def finish(j):
        def pile(i, carry):
            at = pl.ds(pl.multiple_of(i * 2 * local, 2 * local), 2 * local)
            for t in range(width // 128):
                piled[t, at] = jnp.concatenate([recv[2 * i, j, t], recv[2 * i + 1, j, t]], axis=0)
            return carry

        lax.fori_loop(0, half_devices, pile, 0)
        for t in range(width // 128):
            at = slice(t * 128, (t + 1) * 128)
            out[j, at] = piled[t].T - total[j, at]

    @pl.when(in_chain)
    def _():
        for s in range(stages):
            for t in range(2):
                @pl.when(me == 2 * s + t)
                def _():
                    x = solved[s].reshape(count, 2 * width)
                    out[0] = x[:, t * width:(t + 1) * width].T

    @pl.when(jnp.logical_not(in_chain))
    def _():
        finish(0)

    for j in range(1, blocks):
        finish(j)

    for c in range(stages):
        @pl.when(2 * c + my_half != me)
        def _():
            first_remote(c).wait_send()

    @pl.when(in_chain)
    def _():
        for k in range(steps - 1):
            @pl.when(k < me)
            def _():
                strip_remote(k).wait_send()
        for s in range(stages):
            @pl.when(s == group)
            def _():
                for i in range(1, groups):
                    across(s, (s + i) % groups).wait_send()

    def a2a_sent(i, carry):
        target = (me + i) % devices

        @pl.when(target < steps)
        def _():
            a2a_lead(target).wait_send()

        @pl.when(target >= steps)
        def _():
            a2a_rest(target).wait_send()

        return carry

    lax.fori_loop(1, devices, a2a_sent, 0)
    for s in range(stages):
        @pl.when(row == 0)
        def _():
            to_partner(s).wait_send()
            for r in range(1, rows):
                upward(s, r).wait_send()

        @pl.when(row > 0)
        def _():
            for i in range(1, cols):
                in_plane(s, i).wait_send()


def per_device(rows, cols, snapshots, panels, diag_inverse):
    local, order = snapshots.shape
    steps, blocks, width, _ = panels.shape
    devices = rows * cols
    groups = cols // 2
    stages = steps // 2
    count = local * devices
    lanes = 128
    snap = snapshots.reshape(local, blocks, devices, width // lanes, lanes).transpose(1, 2, 3, 0, 4)
    f32, bf16 = jnp.float32, jnp.bfloat16
    vmem, dma = pltpu.VMEM, pltpu.SemaphoreType.DMA
    return pl.pallas_call(
        functools.partial(kernel, rows, cols),
        out_shape=jax.ShapeDtypeStruct((blocks, width, count), f32),
        in_specs=[pl.BlockSpec(memory_space=pl.ANY)] * 3,
        out_specs=pl.BlockSpec(memory_space=pltpu.VMEM),
        scratch_shapes=[
            vmem((devices, blocks, width // lanes, local, lanes), f32),
            vmem((devices // 2, 2, width // lanes, local, lanes), f32),
            vmem((stages, cols, count // cols, 2 * width), f32),
            vmem((2, steps, width, width), f32),
            vmem((stages - 1, 2 * width, 2 * width), bf16),
            vmem((stages - 1, 2 * width, 2 * width), bf16),
            vmem((2 * width, 2 * width), bf16),
            vmem((2 * width, 2 * width), bf16),
            vmem((2, width, width), f32),
            vmem((count // 2, 2 * width), f32),
            vmem((steps, blocks, width, width), f32),
            vmem((stages, blocks, width, 2 * width), bf16),
            vmem((stages, blocks, width, 2 * width), bf16),
            vmem((2 * count, 2 * width), bf16),
            vmem((blocks, width, count), f32),
            vmem((width // lanes, count, lanes), f32),
            dma((devices,)), dma((devices,)),
            dma((stages,)), dma((devices // 2,)),
            dma((steps,)), dma((steps,)), dma((steps,)), dma(()),
            dma((steps,)),
            dma((groups,)), dma((stages, 2)), dma((stages,)), dma((stages, rows - 1)),
            dma((stages, cols)), dma((stages, cols - 1)),
        ],
        compiler_params=pltpu.CompilerParams(
            collective_id=0, has_side_effects=True, vmem_limit_bytes=58 * 1024 * 1024
        ),
        cost_estimate=pl.CostEstimate(
            flops=6 * steps * blocks * width * width * count,
            bytes_accessed=4 * steps * blocks * width * width,
            transcendentals=0,
        ),
    )(snap, panels, diag_inverse)


def solution(mesh):
    in_specs = (P(("row", "col"), None), P(None, None, ("row", "col"), None), P())
    out_specs = P(None, ("row", "col"), None)
    body = functools.partial(per_device, mesh.shape["row"], mesh.shape["col"])
    return jax.shard_map(
        body, mesh=mesh, in_specs=in_specs, out_specs=out_specs, check_vma=False
    )
```

time: 1060 us -> 59.3 us (0.06)
  waiting for transfers between devices: 991 us -> 0 us
  Pallas kernels: 0 us -> 57 us
  matrix products: 41 us -> 0 us
  between operations: 13.7 us -> 0.01 us
    psum x8 -> x0, waiting for transfers between devices: 973 us -> none  [spread(): return lax.psum(block, axis)]
    pallas_call x0 -> x1, Pallas kernels: none -> 57 us  [per_device(): pl.pallas_call(functools.partial(kernel, rows, cols), out_shape=jax.Shape...]
    dot_general x16 -> x0, matrix products: 41 us -> none  [the longest x8 25 us: per_device(): jnp.einsum('jrc,cs->jrs', panels[section], solved, precision=lax.Precisio...]
    all_to_all x1 -> x0, waiting for transfers between devices: 18 us -> none  [per_device(): lax.all_to_all(pieces, ('row', 'col'), split_axis=2, concat_axis=0, tiled...]
  transfers between devices with their start and end apart: 9 -> 0, of which waited for: 9 -> 0; matrix products, arithmetic and copies ran while one was open for 0% -> 0% of each run, Pallas kernels for 0% -> 0%
where the time goes in v1:
time: 59.3 us; the launch traced here: 59.1 us
  Pallas kernels  57 us (96%)
  local copies, waits for them, and re-layouts  2.06 us (3%)
    pallas_call x1, Pallas kernels, per_device(): pl.pallas_call(functools.partial(kernel, rows, cols), out_shape=jax.Shape...  57 us
    unnamed x1, local copies, waits for them, and re-layouts  2.06 us

profile of v1, /device:TPU:25, one launch (start us, length us, event | category | flops | bytes accessed | tf_op | source)
XLA Modules:
  0.0 59.1 jit_solution(15449017870315754026)
XLA Ops:
  0.0 57.0 %shard_map.37 = f32[6,256,128]{2,1,0:T(8,128)} custom-call(f32[6,32,2,4,128]{4,3,2,1,0:T(4,128)} %bitcast.3, f32[8,6,256,256]{3,2,1,0:T(8,128)} %panels.1, f32[8,256,256]{2,1,0:T(8,128)} %diag.1), custom_call_target="tpu_custom_call" | custom-call | flops 2415919104 | bytes 12582912 | tf_op jit(solution)/shard_map/pallas_call | solution.py:426
  57.0 2.1 %copy.5 = f32[6,256,128]{2,1,0:T(8,128)} copy(f32[6,256,128]{2,1,0:T(8,128)} %shard_map.37) | data formatting | bytes 1572864

commit v2 on v1

--- a/solution.py
+++ b/solution.py
@@ -81,9 +81,6 @@
             def _():
                 strip_local(k).start()
 
-    for k in range(steps):
-        staged_copy(k).start()
-
     barrier = pltpu.get_barrier_semaphore()
 
     def greet(i, carry):
@@ -132,6 +129,9 @@
             def _():
                 strip_remote(k).start()
 
+    for k in range(steps):
+        staged_copy(k).start()
+
     def a2a_lead(target):
         return remote(
             snap.at[pl.ds(1, blocks - 1), target], recv.at[me, pl.ds(1, blocks - 1)],
@@ -144,7 +144,7 @@
         )
 
     def a2a_start(i, carry):
-        target = (me + i) % devices
+        target = (me + 1 + (i + devices // 2 - cols // 2) % (devices - 1)) % devices
 
         @pl.when(target < steps)
         def _():
@@ -156,7 +156,15 @@
 
         return carry
 
-    lax.fori_loop(1, devices, a2a_start, 0)
+    def send_rest():
+        lax.fori_loop(0, devices - 1, a2a_start, 0)
+
+    first_group = jnp.logical_and(in_chain, group == 0)
+
+    @pl.when(jnp.logical_not(first_group))
+    def _():
+        send_rest()
+
     own_copy = pltpu.make_async_copy(snap.at[:, me], recv.at[me], a2a_recv.at[me])
     own_copy.start()
 
@@ -181,10 +189,14 @@
 
     mine = side * groups + group
 
-    def to_partner(s):
-        return remote(
-            half_ref(s, side), half_ref(s, side), partner_send.at[s],
-            half_recv.at[s, side], partner,
+    def full(s, g):
+        return jnp.logical_and(g > s, g < stages)
+
+    def to_partner(s, q):
+        piece = side * groups + q
+        return remote(
+            solved.at[s, piece], solved.at[s, piece], partner_send.at[s, q],
+            piece_recv.at[s, piece], partner,
         )
 
     def upward(s, r):
@@ -193,23 +205,45 @@
             piece_recv.at[s, mine], (r, col),
         )
 
+    def in_plane(s, i):
+        g = (group + i) % groups
+        return remote(
+            solved.at[s, mine], solved.at[s, mine], plane_send.at[s, i - 1],
+            piece_recv.at[s, mine], (row, 2 * g + side),
+        )
+
+    def own_piece(s, act):
+        @pl.when(row == 0)
+        def _():
+            for r in range(1, rows):
+                act(upward(s, r))
+
+        for i in range(1, groups):
+            g = (group + i) % groups
+            has = jnp.logical_or(full(s, g), g == s)
+
+            @pl.when(jnp.logical_not(jnp.logical_and(row == 0, has)))
+            def _():
+                act(in_plane(s, i))
+
     def forward(s):
-        for r in range(1, rows):
-            upward(s, r).start()
-        to_partner(s).start()
-
-    def across(s, g):
-        return remote(
-            half_ref(s, side), half_ref(s, side), half_send.at[g],
-            half_recv.at[s, side], (row, 2 * g + side),
-        )
-
-    def in_plane(s, i):
-        target = (col + i) % cols
-        return remote(
-            solved.at[s, mine], solved.at[s, mine], plane_send.at[s, i - 1],
-            piece_recv.at[s, mine], (row, target),
-        )
+        own_piece(s, lambda copy: copy.start())
+        for q in range(groups):
+            to_partner(s, q).start()
+
+    def across(s, i, act):
+        g = (s + i) % groups
+        if s < g < stages:
+            act(remote(
+                half_ref(s, side), half_ref(s, side), half_send.at[i - 1],
+                half_recv.at[s, side], (row, 2 * g + side),
+            ))
+        else:
+            piece = side * groups + g
+            act(remote(
+                solved.at[s, piece], solved.at[s, piece], half_send.at[i - 1],
+                piece_recv.at[s, piece], (row, 2 * g + side),
+            ))
 
     @pl.when(early)
     def _():
@@ -271,7 +305,11 @@
             @pl.when(s < group)
             def _():
                 arrived(half_ref(s, side), half_recv.at[s, side])
-                forward(s)
+
+                @pl.when(s + 1 < group)
+                def _():
+                    forward(s)
+
                 x = half_ref(s, side)[...].reshape(half_count, 2 * width)
                 lead[...] -= product(x, strip_high[min(s, stages - 2)], strip_low[min(s, stages - 2)], NT)
 
@@ -280,32 +318,34 @@
                 x = product(lead[...], inverse_high[...], inverse_low[...], NT)
                 half_ref(s, side)[...] = x.reshape(groups, half_count // groups, 2 * width)
                 for i in range(1, groups):
-                    across(s, (s + i) % groups).start()
+                    across(s, i, lambda copy: copy.start())
+                if s > 0:
+                    forward(s - 1)
                 forward(s)
+                if s == 0:
+                    send_rest()
 
     @pl.when(jnp.logical_not(early))
     def _():
         split_all()
 
-    for s in range(stages):
-        @pl.when(row == 0)
-        def _():
-            @pl.when(jnp.logical_or(jnp.logical_not(in_chain), s > group))
-            def _():
-                arrived(half_ref(s, side), half_recv.at[s, side])
-                forward(s)
-
-            arrived(half_ref(s, 1 - side), half_recv.at[s, 1 - side])
-
-        @pl.when(row > 0)
+    def update_with(s):
+        holds = jnp.logical_and(row == 0, jnp.logical_and(in_chain, s <= group))
+
+        @pl.when(jnp.logical_not(holds))
         def _():
             arrived(solved.at[s, mine], piece_recv.at[s, mine])
-            for i in range(1, cols):
-                in_plane(s, i).start()
-            for i in range(1, cols):
-                other = (col + i) % cols
-                piece = (other % 2) * groups + other // 2
+            own_piece(s, lambda copy: copy.start())
+            to_partner(s, group).start()
+            for i in range(1, groups):
+                q = (group + i) % groups
+                piece = side * groups + q
                 arrived(solved.at[s, piece], piece_recv.at[s, piece])
+                to_partner(s, q).start()
+
+        for q in range(groups):
+            piece = (1 - side) * groups + q
+            arrived(solved.at[s, piece], piece_recv.at[s, piece])
 
         x_high, x_low = halves(solved[s].reshape(count, 2 * width))
         both[:count] = x_high
@@ -317,11 +357,16 @@
             term = a[:, :count] + (a[:, count:] + b)
             if s == 0:
                 total[j] = term
+            elif s < stages - 1:
+                total[j] += term
             else:
-                total[j] += term
+                out[j] -= term
             return carry
 
         lax.fori_loop(0, blocks, update, 0)
+
+    for s in range(stages - 1):
+        update_with(s)
 
     own_copy.wait()
 
@@ -352,6 +397,19 @@
             at = slice(t * 128, (t + 1) * 128)
             out[j, at] = piled[t].T - total[j, at]
 
+    @pl.when(jnp.logical_not(in_chain))
+    def _():
+        finish(0)
+
+    @pl.when(in_chain)
+    def _():
+        out[0] = jnp.zeros_like(out[0])
+
+    for j in range(1, blocks):
+        finish(j)
+
+    update_with(stages - 1)
+
     @pl.when(in_chain)
     def _():
         for s in range(stages):
@@ -361,13 +419,6 @@
                     x = solved[s].reshape(count, 2 * width)
                     out[0] = x[:, t * width:(t + 1) * width].T
 
-    @pl.when(jnp.logical_not(in_chain))
-    def _():
-        finish(0)
-
-    for j in range(1, blocks):
-        finish(j)
-
     for c in range(stages):
         @pl.when(2 * c + my_half != me)
         def _():
@@ -383,7 +434,7 @@
             @pl.when(s == group)
             def _():
                 for i in range(1, groups):
-                    across(s, (s + i) % groups).wait_send()
+                    across(s, i, lambda copy: copy.wait_send())
 
     def a2a_sent(i, carry):
         target = (me + i) % devices
@@ -400,16 +451,9 @@
 
     lax.fori_loop(1, devices, a2a_sent, 0)
     for s in range(stages):
-        @pl.when(row == 0)
-        def _():
-            to_partner(s).wait_send()
-            for r in range(1, rows):
-                upward(s, r).wait_send()
-
-        @pl.when(row > 0)
-        def _():
-            for i in range(1, cols):
-                in_plane(s, i).wait_send()
+        own_piece(s, lambda copy: copy.wait_send())
+        for q in range(groups):
+            to_partner(s, q).wait_send()
 
 
 def per_device(rows, cols, snapshots, panels, diag_inverse):
@@ -449,8 +493,8 @@
             dma((stages,)), dma((devices // 2,)),
             dma((steps,)), dma((steps,)), dma((steps,)), dma(()),
             dma((steps,)),
-            dma((groups,)), dma((stages, 2)), dma((stages,)), dma((stages, rows - 1)),
-            dma((stages, cols)), dma((stages, cols - 1)),
+            dma((groups,)), dma((stages, 2)), dma((stages, groups)), dma((stages, rows - 1)),
+            dma((stages, cols)), dma((stages, groups - 1)),
         ],
         compiler_params=pltpu.CompilerParams(
             collective_id=0, has_side_effects=True, vmem_limit_bytes=58 * 1024 * 1024

time: 59.3 us -> 59.4 us (level)
  no operation moved by 1% of the time
where the time goes in v2:
time: 59.4 us; the launch traced here: 59.2 us
  Pallas kernels  57.1 us (96%)
  local copies, waits for them, and re-layouts  2.06 us (3%)
    pallas_call x1, Pallas kernels, per_device(): pl.pallas_call(functools.partial(kernel, rows, cols), out_shape=jax.Shape...  57.1 us
    unnamed x1, local copies, waits for them, and re-layouts  2.06 us

profile of v2, /device:TPU:25, one launch (start us, length us, event | category | flops | bytes accessed | tf_op | source)
XLA Modules:
  0.0 59.2 jit_solution(748312165641473791)
XLA Ops:
  0.0 57.1 %shard_map.37 = f32[6,256,128]{2,1,0:T(8,128)} custom-call(f32[6,32,2,4,128]{4,3,2,1,0:T(4,128)} %bitcast.3, f32[8,6,256,256]{3,2,1,0:T(8,128)} %panels.1, f32[8,256,256]{2,1,0:T(8,128)} %diag.1), custom_call_target="tpu_custom_call" | custom-call | flops 2415919104 | bytes 12582912 | tf_op jit(solution)/shard_map/pallas_call | solution.py:470
  57.1 2.1 %copy.5 = f32[6,256,128]{2,1,0:T(8,128)} copy(f32[6,256,128]{2,1,0:T(8,128)} %shard_map.37) | data formatting | bytes 1572864

commit v3 on v2

--- a/solution.py
+++ b/solution.py
@@ -31,10 +31,11 @@
 
 def kernel(
     rows, cols, snap, panels, diag, out,
-    recv, first, solved, strip, strip_high, strip_low, inverse_high, inverse_low,
+    packed, recv, first, solved, strip, strip_high, strip_low, inverse_high, inverse_low,
     diagonal, lead, staged, high, low, both, total, piled,
     a2a_send, a2a_recv, first_send, first_recv, strip_send, strip_recv, strip_own, diag_sem,
     staged_sem, half_send, half_recv, partner_send, up_send, piece_recv, plane_send,
+    pack_sem,
 ):
     devices = rows * cols
     groups = cols // 2
@@ -73,6 +74,12 @@
     def staged_copy(k):
         return pltpu.make_async_copy(panels.at[k], staged.at[k], staged_sem.at[k])
 
+    def pack(j):
+        return pltpu.make_async_copy(snap.at[j], packed.at[:, j], pack_sem.at[j])
+
+    for j in range(blocks):
+        pack(j).start()
+
     @pl.when(in_chain)
     def _():
         diag_copy().start()
@@ -90,6 +97,8 @@
         return carry
 
     lax.fori_loop(1, devices, greet, 0)
+    for j in range(blocks):
+        pack(j).wait()
     pl.semaphore_wait(barrier, devices - 1)
 
     my_half = me // half_devices
@@ -97,13 +106,13 @@
 
     def first_remote(c):
         return remote(
-            snap.at[0, pl.ds(2 * c, 2)], first.at[place], first_send.at[c],
+            packed.at[pl.ds(2 * c, 2), 0], first.at[place], first_send.at[c],
             first_recv.at[place], device(2 * c + my_half),
         )
 
     def first_local(c):
         return pltpu.make_async_copy(
-            snap.at[0, pl.ds(2 * c, 2)], first.at[place], first_recv.at[place]
+            packed.at[pl.ds(2 * c, 2), 0], first.at[place], first_recv.at[place]
         )
 
     for c in range(stages):
@@ -134,13 +143,13 @@
 
     def a2a_lead(target):
         return remote(
-            snap.at[pl.ds(1, blocks - 1), target], recv.at[me, pl.ds(1, blocks - 1)],
+            packed.at[target, pl.ds(1, blocks - 1)], recv.at[me, pl.ds(1, blocks - 1)],
             a2a_send.at[target], a2a_recv.at[me], device(target),
         )
 
     def a2a_rest(target):
         return remote(
-            snap.at[:, target], recv.at[me], a2a_send.at[target], a2a_recv.at[me], device(target)
+            packed.at[target], recv.at[me], a2a_send.at[target], a2a_recv.at[me], device(target)
         )
 
     def a2a_start(i, carry):
@@ -159,13 +168,13 @@
     def send_rest():
         lax.fori_loop(0, devices - 1, a2a_start, 0)
 
-    first_group = jnp.logical_and(in_chain, group == 0)
-
-    @pl.when(jnp.logical_not(first_group))
+    waiting = me < steps // 2
+
+    @pl.when(jnp.logical_not(waiting))
     def _():
         send_rest()
 
-    own_copy = pltpu.make_async_copy(snap.at[:, me], recv.at[me], a2a_recv.at[me])
+    own_copy = pltpu.make_async_copy(packed.at[me], recv.at[me], a2a_recv.at[me])
     own_copy.start()
 
     def split_all():
@@ -199,10 +208,10 @@
             piece_recv.at[s, piece], partner,
         )
 
-    def upward(s, r):
-        return remote(
-            solved.at[s, mine], solved.at[s, mine], up_send.at[s, r - 1],
-            piece_recv.at[s, mine], (r, col),
+    def upward(s):
+        return remote(
+            solved.at[s, mine], solved.at[s, mine], up_send.at[s],
+            piece_recv.at[s, mine], (row + 1, col),
         )
 
     def in_plane(s, i):
@@ -213,10 +222,9 @@
         )
 
     def own_piece(s, act):
-        @pl.when(row == 0)
-        def _():
-            for r in range(1, rows):
-                act(upward(s, r))
+        @pl.when(row < rows - 1)
+        def _():
+            act(upward(s))
 
         for i in range(1, groups):
             g = (group + i) % groups
@@ -322,21 +330,26 @@
                 if s > 0:
                     forward(s - 1)
                 forward(s)
-                if s == 0:
+                if 2 * s < steps // 2:
                     send_rest()
 
     @pl.when(jnp.logical_not(early))
     def _():
         split_all()
 
-    def update_with(s):
-        holds = jnp.logical_and(row == 0, jnp.logical_and(in_chain, s <= group))
-
-        @pl.when(jnp.logical_not(holds))
+    def holds(s):
+        return jnp.logical_and(row == 0, jnp.logical_and(in_chain, s <= group))
+
+    def pass_on(s):
+        @pl.when(jnp.logical_not(holds(s)))
         def _():
             arrived(solved.at[s, mine], piece_recv.at[s, mine])
             own_piece(s, lambda copy: copy.start())
             to_partner(s, group).start()
+
+    def update_with(s):
+        @pl.when(jnp.logical_not(holds(s)))
+        def _():
             for i in range(1, groups):
                 q = (group + i) % groups
                 piece = side * groups + q
@@ -366,7 +379,9 @@
         lax.fori_loop(0, blocks, update, 0)
 
     for s in range(stages - 1):
+        pass_on(s)
         update_with(s)
+    pass_on(stages - 1)
 
     own_copy.wait()
 
@@ -473,6 +488,7 @@
         in_specs=[pl.BlockSpec(memory_space=pl.ANY)] * 3,
         out_specs=pl.BlockSpec(memory_space=pltpu.VMEM),
         scratch_shapes=[
+            vmem((devices, blocks, width // lanes, local, lanes), f32),
             vmem((devices, blocks, width // lanes, local, lanes), f32),
             vmem((devices // 2, 2, width // lanes, local, lanes), f32),
             vmem((stages, cols, count // cols, 2 * width), f32),
@@ -493,8 +509,9 @@
             dma((stages,)), dma((devices // 2,)),
             dma((steps,)), dma((steps,)), dma((steps,)), dma(()),
             dma((steps,)),
-            dma((groups,)), dma((stages, 2)), dma((stages, groups)), dma((stages, rows - 1)),
+            dma((groups,)), dma((stages, 2)), dma((stages, groups)), dma((stages,)),
             dma((stages, cols)), dma((stages, groups - 1)),
+            dma((blocks,)),
         ],
         compiler_params=pltpu.CompilerParams(
             collective_id=0, has_side_effects=True, vmem_limit_bytes=58 * 1024 * 1024

time: 59.4 us -> 61.9 us (1.042)
  Pallas kernels: 57.1 us -> 59.6 us
    pallas_call x1, Pallas kernels: 57.1 us -> 59.6 us  [per_device(): pl.pallas_call(functools.partial(kernel, rows, cols), out_shape=jax.Shape...]
where the time goes in v3:
time: 61.9 us; the launch traced here: 61.7 us
  Pallas kernels  59.6 us (96%)
  local copies, waits for them, and re-layouts  2.06 us (3%)
    pallas_call x1, Pallas kernels, per_device(): pl.pallas_call(functools.partial(kernel, rows, cols), out_shape=jax.Shape...  59.6 us
    unnamed x1, local copies, waits for them, and re-layouts  2.06 us

profile of v3, /device:TPU:25, one launch (start us, length us, event | category | flops | bytes accessed | tf_op | source)
XLA Modules:
  0.0 61.7 jit_solution(1827550814516730361)
XLA Ops:
  0.0 59.6 %shard_map.37 = f32[6,256,128]{2,1,0:T(8,128)} custom-call(f32[6,32,2,4,128]{4,3,2,1,0:T(4,128)} %bitcast.3, f32[8,6,256,256]{3,2,1,0:T(8,128)} %panels.1, f32[8,256,256]{2,1,0:T(8,128)} %diag.1), custom_call_target="tpu_custom_call" | custom-call | flops 2415919104 | bytes 12582912 | tf_op jit(solution)/shard_map/pallas_call | solution.py:485
  59.6 2.1 %copy.5 = f32[6,256,128]{2,1,0:T(8,128)} copy(f32[6,256,128]{2,1,0:T(8,128)} %shard_map.37) | data formatting | bytes 1572864

commit v4 on v3

--- a/solution.py
+++ b/solution.py
@@ -35,7 +35,7 @@
     diagonal, lead, staged, high, low, both, total, piled,
     a2a_send, a2a_recv, first_send, first_recv, strip_send, strip_recv, strip_own, diag_sem,
     staged_sem, half_send, half_recv, partner_send, up_send, piece_recv, plane_send,
-    pack_sem,
+    pack_sem, swap_send, swap_recv,
 ):
     devices = rows * cols
     groups = cols // 2
@@ -43,7 +43,7 @@
     stages = steps // 2
     count = out.shape[2]
     half_count = count // 2
-    local = snap.shape[3]
+    local = snap.shape[4]
     half_devices = devices // 2
 
     row = lax.axis_index("row")
@@ -75,7 +75,9 @@
         return pltpu.make_async_copy(panels.at[k], staged.at[k], staged_sem.at[k])
 
     def pack(j):
-        return pltpu.make_async_copy(snap.at[j], packed.at[:, j], pack_sem.at[j])
+        return pltpu.make_async_copy(
+            snap.at[j, :, side], packed.at[j, :, side], pack_sem.at[j]
+        )
 
     for j in range(blocks):
         pack(j).start()
@@ -97,8 +99,6 @@
         return carry
 
     lax.fori_loop(1, devices, greet, 0)
-    for j in range(blocks):
-        pack(j).wait()
     pl.semaphore_wait(barrier, devices - 1)
 
     my_half = me // half_devices
@@ -106,13 +106,13 @@
 
     def first_remote(c):
         return remote(
-            packed.at[pl.ds(2 * c, 2), 0], first.at[place], first_send.at[c],
+            snap.at[0, c], first.at[place], first_send.at[c],
             first_recv.at[place], device(2 * c + my_half),
         )
 
     def first_local(c):
         return pltpu.make_async_copy(
-            packed.at[pl.ds(2 * c, 2), 0], first.at[place], first_recv.at[place]
+            snap.at[0, c], first.at[place], first_recv.at[place]
         )
 
     for c in range(stages):
@@ -131,51 +131,77 @@
             panels.at[k, 0], strip.at[side, k], strip_send.at[k], strip_recv.at[k], partner
         )
 
-    @pl.when(in_chain)
-    def _():
+    def strips():
         for k in reversed(range(steps - 1)):
             @pl.when(k < me)
             def _():
                 strip_remote(k).start()
 
+    @pl.when(me < 2)
+    def _():
+        strips()
+
+    def swap(j):
+        return remote(
+            snap.at[j, :, 1 - side], packed.at[j, :, side], swap_send.at[j], swap_recv.at[j],
+            partner,
+        )
+
+    for j in range(blocks):
+        swap(j).start()
+
+    @pl.when(jnp.logical_and(in_chain, me >= 2))
+    def _():
+        strips()
+
     for k in range(steps):
         staged_copy(k).start()
 
-    def a2a_lead(target):
-        return remote(
-            packed.at[target, pl.ds(1, blocks - 1)], recv.at[me, pl.ds(1, blocks - 1)],
-            a2a_send.at[target], a2a_recv.at[me], device(target),
-        )
-
-    def a2a_rest(target):
-        return remote(
-            packed.at[target], recv.at[me], a2a_send.at[target], a2a_recv.at[me], device(target)
-        )
+    pair = me // 2
+    pairs = devices // 2
+
+    def a2a_lead(to):
+        return remote(
+            packed.at[pl.ds(1, blocks - 1), to],
+            recv.at[pl.ds(1, blocks - 1), pl.ds(2 * pair, 2)],
+            a2a_send.at[to], a2a_recv.at[pair], device(2 * to + side),
+        )
+
+    def a2a_rest(to):
+        return remote(
+            packed.at[:, to], recv.at[:, pl.ds(2 * pair, 2)],
+            a2a_send.at[to], a2a_recv.at[pair], device(2 * to + side),
+        )
+
+    own_copy = pltpu.make_async_copy(
+        packed.at[:, pair], recv.at[:, pl.ds(2 * pair, 2)], a2a_recv.at[pair]
+    )
 
     def a2a_start(i, carry):
-        target = (me + 1 + (i + devices // 2 - cols // 2) % (devices - 1)) % devices
-
-        @pl.when(target < steps)
-        def _():
-            a2a_lead(target).start()
-
-        @pl.when(target >= steps)
-        def _():
-            a2a_rest(target).start()
+        to = (pair + 1 + (i + pairs // 2 - groups // 2) % (pairs - 1)) % pairs
+
+        @pl.when(2 * to < steps)
+        def _():
+            a2a_lead(to).start()
+
+        @pl.when(2 * to >= steps)
+        def _():
+            a2a_rest(to).start()
 
         return carry
 
     def send_rest():
-        lax.fori_loop(0, devices - 1, a2a_start, 0)
+        for j in range(blocks):
+            pack(j).wait()
+            arrived(packed.at[j, :, 1 - side], swap_recv.at[j])
+        lax.fori_loop(0, pairs - 1, a2a_start, 0)
+        own_copy.start()
 
     waiting = me < steps // 2
 
     @pl.when(jnp.logical_not(waiting))
     def _():
         send_rest()
-
-    own_copy = pltpu.make_async_copy(packed.at[me], recv.at[me], a2a_recv.at[me])
-    own_copy.start()
 
     def split_all():
         for k in range(steps):
@@ -208,10 +234,10 @@
             piece_recv.at[s, piece], partner,
         )
 
-    def upward(s):
-        return remote(
-            solved.at[s, mine], solved.at[s, mine], up_send.at[s],
-            piece_recv.at[s, mine], (row + 1, col),
+    def upward(s, r):
+        return remote(
+            solved.at[s, mine], solved.at[s, mine], up_send.at[s, r - 1],
+            piece_recv.at[s, mine], (row + r, col),
         )
 
     def in_plane(s, i):
@@ -222,9 +248,15 @@
         )
 
     def own_piece(s, act):
-        @pl.when(row < rows - 1)
-        def _():
-            act(upward(s))
+        if s < stages - 1:
+            @pl.when(row < rows - 1)
+            def _():
+                act(upward(s, 1))
+        else:
+            @pl.when(row == 0)
+            def _():
+                for r in range(1, rows):
+                    act(upward(s, r))
 
         for i in range(1, groups):
             g = (group + i) % groups
@@ -386,25 +418,25 @@
     own_copy.wait()
 
     def a2a_wait(i, carry):
-        source = (me + i) % devices
+        source = (pair + i) % pairs
 
         @pl.when(in_chain)
         def _():
-            arrived(recv.at[source, pl.ds(1, blocks - 1)], a2a_recv.at[source])
+            arrived(recv.at[pl.ds(1, blocks - 1), pl.ds(2 * source, 2)], a2a_recv.at[source])
 
         @pl.when(jnp.logical_not(in_chain))
         def _():
-            arrived(recv.at[source], a2a_recv.at[source])
+            arrived(recv.at[:, pl.ds(2 * source, 2)], a2a_recv.at[source])
 
         return carry
 
-    lax.fori_loop(1, devices, a2a_wait, 0)
+    lax.fori_loop(1, pairs, a2a_wait, 0)
 
     def finish(j):
         def pile(i, carry):
             at = pl.ds(pl.multiple_of(i * 2 * local, 2 * local), 2 * local)
             for t in range(width // 128):
-                piled[t, at] = jnp.concatenate([recv[2 * i, j, t], recv[2 * i + 1, j, t]], axis=0)
+                piled[t, at] = jnp.concatenate([recv[j, 2 * i, t], recv[j, 2 * i + 1, t]], axis=0)
             return carry
 
         lax.fori_loop(0, half_devices, pile, 0)
@@ -452,19 +484,21 @@
                     across(s, i, lambda copy: copy.wait_send())
 
     def a2a_sent(i, carry):
-        target = (me + i) % devices
-
-        @pl.when(target < steps)
-        def _():
-            a2a_lead(target).wait_send()
-
-        @pl.when(target >= steps)
-        def _():
-            a2a_rest(target).wait_send()
+        to = (pair + i) % pairs
+
+        @pl.when(2 * to < steps)
+        def _():
+            a2a_lead(to).wait_send()
+
+        @pl.when(2 * to >= steps)
+        def _():
+            a2a_rest(to).wait_send()
 
         return carry
 
-    lax.fori_loop(1, devices, a2a_sent, 0)
+    lax.fori_loop(1, pairs, a2a_sent, 0)
+    for j in range(blocks):
+        swap(j).wait_send()
     for s in range(stages):
         own_piece(s, lambda copy: copy.wait_send())
         for q in range(groups):
@@ -479,7 +513,8 @@
     stages = steps // 2
     count = local * devices
     lanes = 128
-    snap = snapshots.reshape(local, blocks, devices, width // lanes, lanes).transpose(1, 2, 3, 0, 4)
+    snap = snapshots.reshape(local, blocks, devices // 2, 2, width // lanes, lanes)
+    snap = snap.transpose(1, 2, 3, 4, 0, 5)
     f32, bf16 = jnp.float32, jnp.bfloat16
     vmem, dma = pltpu.VMEM, pltpu.SemaphoreType.DMA
     return pl.pallas_call(
@@ -488,8 +523,8 @@
         in_specs=[pl.BlockSpec(memory_space=pl.ANY)] * 3,
         out_specs=pl.BlockSpec(memory_space=pltpu.VMEM),
         scratch_shapes=[
-            vmem((devices, blocks, width // lanes, local, lanes), f32),
-            vmem((devices, blocks, width // lanes, local, lanes), f32),
+            vmem((blocks, devices // 2, 2, width // lanes, local, lanes), f32),
+            vmem((blocks, devices, width // lanes, local, lanes), f32),
             vmem((devices // 2, 2, width // lanes, local, lanes), f32),
             vmem((stages, cols, count // cols, 2 * width), f32),
             vmem((2, steps, width, width), f32),
@@ -505,13 +540,13 @@
             vmem((2 * count, 2 * width), bf16),
             vmem((blocks, width, count), f32),
             vmem((width // lanes, count, lanes), f32),
-            dma((devices,)), dma((devices,)),
+            dma((devices // 2,)), dma((devices // 2,)),
             dma((stages,)), dma((devices // 2,)),
             dma((steps,)), dma((steps,)), dma((steps,)), dma(()),
             dma((steps,)),
-            dma((groups,)), dma((stages, 2)), dma((stages, groups)), dma((stages,)),
+            dma((groups,)), dma((stages, 2)), dma((stages, groups)), dma((stages, rows - 1)),
             dma((stages, cols)), dma((stages, groups - 1)),
-            dma((blocks,)),
+            dma((blocks,)), dma((blocks,)), dma((blocks,)),
         ],
         compiler_params=pltpu.CompilerParams(
             collective_id=0, has_side_effects=True, vmem_limit_bytes=58 * 1024 * 1024

time: 61.9 us -> 61.1 us (0.987)
  Pallas kernels: 59.6 us -> 58.8 us
    pallas_call x1, Pallas kernels: 59.6 us -> 58.8 us  [per_device(): pl.pallas_call(functools.partial(kernel, rows, cols), out_shape=jax.Shape...]
where the time goes in v4:
time: 61.1 us; the launch traced here: 60.9 us
  Pallas kernels  58.8 us (96%)
  local copies, waits for them, and re-layouts  2.06 us (3%)
    pallas_call x1, Pallas kernels, per_device(): pl.pallas_call(functools.partial(kernel, rows, cols), out_shape=jax.Shape...  58.8 us
    unnamed x1, local copies, waits for them, and re-layouts  2.06 us

profile of v4, /device:TPU:25, one launch (start us, length us, event | category | flops | bytes accessed | tf_op | source)
XLA Modules:
  0.0 60.9 jit_solution(6208598483675486491)
XLA Ops:
  0.0 58.8 %shard_map.37 = f32[6,256,128]{2,1,0:T(8,128)} custom-call(f32[6,16,2,2,4,128]{5,4,3,2,1,0:T(4,128)} %bitcast.3, f32[8,6,256,256]{3,2,1,0:T(8,128)} %panels.1, f32[8,256,256]{2,1,0:T(8,128)} %diag.1), custom_call_target="tpu_custom_call" | custom-call | flops 2415919104 | bytes 12582912 | tf_op jit(solution)/shard_map/pallas_call | solution.py:520
  58.9 2.1 %copy.5 = f32[6,256,128]{2,1,0:T(8,128)} copy(f32[6,256,128]{2,1,0:T(8,128)} %shard_map.37) | data formatting | bytes 1572864

commit v5 on v4

--- a/solution.py
+++ b/solution.py
@@ -8,8 +8,6 @@
 from jax.sharding import PartitionSpec as P
 
 MESH = pl.DeviceIdType.MESH
-NT = (((1,), (1,)), ((), ()))
-NN = (((1,), (0,)), ((), ()))
 
 
 def halves(value):
@@ -18,21 +16,21 @@
     return high, low
 
 
-def mul(a, b, dims):
-    return lax.dot_general(a, b, dims, preferred_element_type=jnp.float32)
-
-
-def product(a, b_high, b_low, dims):
+def mul(a, b):
+    return jnp.dot(a, b, preferred_element_type=jnp.float32)
+
+
+def product(a, b_high, b_low):
     rows = a.shape[0]
     a_high, a_low = halves(a)
-    both = mul(jnp.concatenate([a_high, a_low], axis=0), b_high, dims)
-    return both[:rows] + (both[rows:] + mul(a_high, b_low, dims))
+    both = mul(jnp.concatenate([a_high, a_low], axis=0), b_high)
+    return both[:rows] + (both[rows:] + mul(a_high, b_low))
 
 
 def kernel(
     rows, cols, snap, panels, diag, out,
     packed, recv, first, solved, strip, strip_high, strip_low, inverse_high, inverse_low,
-    diagonal, lead, staged, high, low, both, total, piled,
+    diagonal, lead, staged, high, low, both, total,
     a2a_send, a2a_recv, first_send, first_recv, strip_send, strip_recv, strip_own, diag_sem,
     staged_sem, half_send, half_recv, partner_send, up_send, piece_recv, plane_send,
     pack_sem, swap_send, swap_recv,
@@ -248,15 +246,10 @@
         )
 
     def own_piece(s, act):
-        if s < stages - 1:
-            @pl.when(row < rows - 1)
-            def _():
-                act(upward(s, 1))
-        else:
-            @pl.when(row == 0)
-            def _():
-                for r in range(1, rows):
-                    act(upward(s, r))
+        @pl.when(row == 0)
+        def _():
+            for r in range(1, rows):
+                act(upward(s, r))
 
         for i in range(1, groups):
             g = (group + i) % groups
@@ -304,11 +297,11 @@
         d0, d1 = diagonal[0], diagonal[1]
         d0_high, d0_low = halves(d0)
         below = strip[1, 2 * group]
-        inner = product(below, d0_high, d0_low, NN)
+        inner = product(below, d0_high, d0_low)
         inner_high, inner_low = halves(inner)
-        corner = -product(d1, inner_high, inner_low, NN)
+        corner = -product(d1, inner_high, inner_low)
         for r0, c0, value in (
-            (0, 0, d0), (0, width, jnp.zeros_like(d0)), (width, 0, corner), (width, width, d1)
+            (0, 0, d0.T), (width, 0, jnp.zeros_like(d0)), (0, width, corner.T), (width, width, d1.T)
         ):
             h, l = halves(value)
             inverse_high[r0:r0 + width, c0:c0 + width] = h
@@ -318,8 +311,8 @@
             def _():
                 for b in range(2):
                     for t in range(2):
-                        h, l = halves(strip[b, 2 * s + t])
-                        place_ = (s, slice(b * width, (b + 1) * width), slice(t * width, (t + 1) * width))
+                        h, l = halves(strip[b, 2 * s + t].T)
+                        place_ = (s, slice(t * width, (t + 1) * width), slice(b * width, (b + 1) * width))
                         strip_high[place_] = h
                         strip_low[place_] = l
 
@@ -329,17 +322,10 @@
 
         lax.fori_loop(0, half_devices, first_wait, 0)
 
-        def pile(i, carry):
-            at = pl.ds(pl.multiple_of(i * 2 * local, 2 * local), 2 * local)
-            for b in range(2):
-                for t in range(width // 128):
-                    lanes = slice(b * width + t * 128, b * width + (t + 1) * 128)
-                    lead[at, lanes] = jnp.concatenate(
-                        [first[2 * i, b, t], first[2 * i + 1, b, t]], axis=0
-                    )
-            return carry
-
-        lax.fori_loop(0, half_devices // 2, pile, 0)
+        for b in range(2):
+            for t in range(width // 128):
+                lanes = slice(b * width + t * 128, b * width + (t + 1) * 128)
+                lead[:, lanes] = first[:, b, t].reshape(half_count, 128)
 
         for s in range(stages):
             @pl.when(s < group)
@@ -351,11 +337,11 @@
                     forward(s)
 
                 x = half_ref(s, side)[...].reshape(half_count, 2 * width)
-                lead[...] -= product(x, strip_high[min(s, stages - 2)], strip_low[min(s, stages - 2)], NT)
+                lead[...] -= product(x, strip_high[min(s, stages - 2)], strip_low[min(s, stages - 2)])
 
             @pl.when(s == group)
             def _():
-                x = product(lead[...], inverse_high[...], inverse_low[...], NT)
+                x = product(lead[...], inverse_high[...], inverse_low[...])
                 half_ref(s, side)[...] = x.reshape(groups, half_count // groups, 2 * width)
                 for i in range(1, groups):
                     across(s, i, lambda copy: copy.start())
@@ -392,14 +378,15 @@
             piece = (1 - side) * groups + q
             arrived(solved.at[s, piece], piece_recv.at[s, piece])
 
-        x_high, x_low = halves(solved[s].reshape(count, 2 * width))
-        both[:count] = x_high
-        both[count:] = x_low
-
-        def update(j, carry):
-            a = mul(high[s, j], both[...], NT)
-            b = mul(low[s, j], both[:count], NT)
-            term = a[:, :count] + (a[:, count:] + b)
+        x_high, x_low = halves(solved[s].reshape(count, 2 * width).T)
+        both[:, :count] = x_high
+        both[:, count:] = x_low
+
+        def update(i, carry):
+            j = pl.ds(2 * i, 2)
+            a = mul(high[s, j].reshape(2 * width, 2 * width), both[...])
+            b = mul(low[s, j].reshape(2 * width, 2 * width), both[:, :count])
+            term = (a[:, :count] + (a[:, count:] + b)).reshape(2, width, count)
             if s == 0:
                 total[j] = term
             elif s < stages - 1:
@@ -408,7 +395,7 @@
                 out[j] -= term
             return carry
 
-        lax.fori_loop(0, blocks, update, 0)
+        lax.fori_loop(0, blocks // 2, update, 0)
 
     for s in range(stages - 1):
         pass_on(s)
@@ -433,16 +420,9 @@
     lax.fori_loop(1, pairs, a2a_wait, 0)
 
     def finish(j):
-        def pile(i, carry):
-            at = pl.ds(pl.multiple_of(i * 2 * local, 2 * local), 2 * local)
-            for t in range(width // 128):
-                piled[t, at] = jnp.concatenate([recv[j, 2 * i, t], recv[j, 2 * i + 1, t]], axis=0)
-            return carry
-
-        lax.fori_loop(0, half_devices, pile, 0)
         for t in range(width // 128):
             at = slice(t * 128, (t + 1) * 128)
-            out[j, at] = piled[t].T - total[j, at]
+            out[j, at] = recv[j, :, t].reshape(count, 128).T - total[j, at]
 
     @pl.when(jnp.logical_not(in_chain))
     def _():
@@ -537,9 +517,8 @@
             vmem((steps, blocks, width, width), f32),
             vmem((stages, blocks, width, 2 * width), bf16),
             vmem((stages, blocks, width, 2 * width), bf16),
-            vmem((2 * count, 2 * width), bf16),
+            vmem((2 * width, 2 * count), bf16),
             vmem((blocks, width, count), f32),
-            vmem((width // lanes, count, lanes), f32),
             dma((devices // 2,)), dma((devices // 2,)),
             dma((stages,)), dma((devices // 2,)),
             dma((steps,)), dma((steps,)), dma((steps,)), dma(()),

time: 61.1 us -> 54.5 us (0.89)
  Pallas kernels: 58.8 us -> 52.3 us
    pallas_call x1, Pallas kernels: 58.8 us -> 52.3 us  [per_device(): pl.pallas_call(functools.partial(kernel, rows, cols), out_shape=jax.Shape...]
where the time goes in v5:
time: 54.5 us; the launch traced here: 54.4 us
  Pallas kernels  52.3 us (96%)
  local copies, waits for them, and re-layouts  2.06 us (4%)
    pallas_call x1, Pallas kernels, per_device(): pl.pallas_call(functools.partial(kernel, rows, cols), out_shape=jax.Shape...  52.3 us
    unnamed x1, local copies, waits for them, and re-layouts  2.06 us

profile of v5, /device:TPU:25, one launch (start us, length us, event | category | flops | bytes accessed | tf_op | source)
XLA Modules:
  0.0 54.4 jit_solution(15532554365723546779)
XLA Ops:
  0.0 52.3 %shard_map.37 = f32[6,256,128]{2,1,0:T(8,128)} custom-call(f32[6,16,2,2,4,128]{5,4,3,2,1,0:T(4,128)} %bitcast.3, f32[8,6,256,256]{3,2,1,0:T(8,128)} %panels.1, f32[8,256,256]{2,1,0:T(8,128)} %diag.1), custom_call_target="tpu_custom_call" | custom-call | flops 2415919104 | bytes 12582912 | tf_op jit(solution)/shard_map/pallas_call | solution.py:500
  52.3 2.1 %copy.5 = f32[6,256,128]{2,1,0:T(8,128)} copy(f32[6,256,128]{2,1,0:T(8,128)} %shard_map.37) | data formatting | bytes 1572864

commit v6 on v5

--- a/solution.py
+++ b/solution.py
@@ -188,18 +188,26 @@
 
         return carry
 
-    def send_rest():
+    def swapped():
         for j in range(blocks):
             pack(j).wait()
             arrived(packed.at[j, :, 1 - side], swap_recv.at[j])
-        lax.fori_loop(0, pairs - 1, a2a_start, 0)
         own_copy.start()
 
-    waiting = me < steps // 2
-
-    @pl.when(jnp.logical_not(waiting))
-    def _():
-        send_rest()
+    others = pairs - 1
+    opening = jnp.where(in_chain, others // 5, 4 * others // 15)
+    until = [(7 + 3 * s) * others // 15 for s in range(stages - 1)] + [others]
+
+    def batch(begin, end):
+        lax.fori_loop(begin, end, a2a_start, 0)
+
+    leads = jnp.logical_and(in_chain, group == 0)
+    opening = jnp.where(leads, 0, opening)
+
+    @pl.when(jnp.logical_not(leads))
+    def _():
+        swapped()
+        batch(0, opening)
 
     def split_all():
         for k in range(steps):
@@ -348,8 +356,9 @@
                 if s > 0:
                     forward(s - 1)
                 forward(s)
-                if 2 * s < steps // 2:
-                    send_rest()
+                if s == 0:
+                    swapped()
+                batch(opening, until[0])
 
     @pl.when(jnp.logical_not(early))
     def _():
@@ -397,10 +406,16 @@
 
         lax.fori_loop(0, blocks // 2, update, 0)
 
-    for s in range(stages - 1):
+    for s in range(stages):
         pass_on(s)
-        update_with(s)
-    pass_on(stages - 1)
+        if s == 0:
+            @pl.when(jnp.logical_not(in_chain))
+            def _():
+                batch(opening, until[0])
+        else:
+            batch(until[s - 1], until[s])
+        if s < stages - 1:
+            update_with(s)
 
     own_copy.wait()
 

time: 54.5 us -> 57.6 us (1.057)
  the two profiles are of different devices: /device:TPU:25 before, /device:TPU:0 now
where the time goes in v6:
time: 57.6 us; the launch traced here: 57.4 us
  Pallas kernels  55.4 us (96%)
  local copies, waits for them, and re-layouts  2.06 us (4%)
    pallas_call x1, Pallas kernels, per_device(): pl.pallas_call(functools.partial(kernel, rows, cols), out_shape=jax.Shape...  55.4 us
    unnamed x1, local copies, waits for them, and re-layouts  2.06 us

profile of v6, /device:TPU:0, one launch (start us, length us, event | category | flops | bytes accessed | tf_op | source)
XLA Modules:
  0.0 57.4 jit_solution(12069193514394146502)
XLA Ops:
  0.0 55.4 %shard_map.37 = f32[6,256,128]{2,1,0:T(8,128)} custom-call(f32[6,16,2,2,4,128]{5,4,3,2,1,0:T(4,128)} %bitcast.3, f32[8,6,256,256]{3,2,1,0:T(8,128)} %panels.1, f32[8,256,256]{2,1,0:T(8,128)} %diag.1), custom_call_target="tpu_custom_call" | custom-call | flops 2415919104 | bytes 12582912 | tf_op jit(solution)/shard_map/pallas_call | solution.py:515
  55.4 2.1 %copy.5 = f32[6,256,128]{2,1,0:T(8,128)} copy(f32[6,256,128]{2,1,0:T(8,128)} %shard_map.37) | data formatting | bytes 1572864

commit v7 on v6

--- a/solution.py
+++ b/solution.py
@@ -195,14 +195,11 @@
         own_copy.start()
 
     others = pairs - 1
-    opening = jnp.where(in_chain, others // 5, 4 * others // 15)
-    until = [(7 + 3 * s) * others // 15 for s in range(stages - 1)] + [others]
+    leads = me < steps // 2
+    opening = jnp.where(leads, 0, jnp.where(in_chain, (others + 1) // 2, others))
 
     def batch(begin, end):
         lax.fori_loop(begin, end, a2a_start, 0)
-
-    leads = jnp.logical_and(in_chain, group == 0)
-    opening = jnp.where(leads, 0, opening)
 
     @pl.when(jnp.logical_not(leads))
     def _():
@@ -356,9 +353,9 @@
                 if s > 0:
                     forward(s - 1)
                 forward(s)
-                if s == 0:
+                if 2 * s < steps // 2:
                     swapped()
-                batch(opening, until[0])
+                batch(opening, others)
 
     @pl.when(jnp.logical_not(early))
     def _():
@@ -408,12 +405,6 @@
 
     for s in range(stages):
         pass_on(s)
-        if s == 0:
-            @pl.when(jnp.logical_not(in_chain))
-            def _():
-                batch(opening, until[0])
-        else:
-            batch(until[s - 1], until[s])
         if s < stages - 1:
             update_with(s)
 

time: 57.6 us -> 54.3 us (0.943)
  the two profiles are of different devices: /device:TPU:0 before, /device:TPU:25 now
where the time goes in v7:
time: 54.3 us; the launch traced here: 54 us
  Pallas kernels  51.9 us (96%)
  local copies, waits for them, and re-layouts  2.06 us (4%)
    pallas_call x1, Pallas kernels, per_device(): pl.pallas_call(functools.partial(kernel, rows, cols), out_shape=jax.Shape...  51.9 us
    unnamed x1, local copies, waits for them, and re-layouts  2.06 us

profile of v7, /device:TPU:25, one launch (start us, length us, event | category | flops | bytes accessed | tf_op | source)
XLA Modules:
  0.0 54.0 jit_solution(8267554400037399564)
XLA Ops:
  0.0 51.9 %shard_map.37 = f32[6,256,128]{2,1,0:T(8,128)} custom-call(f32[6,16,2,2,4,128]{5,4,3,2,1,0:T(4,128)} %bitcast.3, f32[8,6,256,256]{3,2,1,0:T(8,128)} %panels.1, f32[8,256,256]{2,1,0:T(8,128)} %diag.1), custom_call_target="tpu_custom_call" | custom-call | flops 2415919104 | bytes 12582912 | tf_op jit(solution)/shard_map/pallas_call | solution.py:506
  51.9 2.1 %copy.5 = f32[6,256,128]{2,1,0:T(8,128)} copy(f32[6,256,128]{2,1,0:T(8,128)} %shard_map.37) | data formatting | bytes 1572864
